TPU v7x, 32 devices: a whole 2x2x4 slice. The times are simulated.
32 devices in a mesh: row: 4 (over y, core), col: 8 (over z, x).
Axes of the slice: x: 2, y: 2, z: 4, core: 2. Of those that a mesh axis runs over, the one named last changes fastest.
Arguments:
- transition: bfloat16 [32768, 32768], P('row', 'col'), may hold values from 1.5258789e-06 to 0.0024414062, as said below
- emission: bfloat16 [96, 32768], P(None, 'col'), may hold values from 0.0099487305 to 1
- token_ids: int32 [2, 192], replicated, may hold values from 0 to 95
- forward: bfloat16 [2, 192, 32768], P(None, 'col', 'row'), may hold values from 3.0517578e-06 to 0.0008239746, as said below
- backward_last: float32 [192, 32768], P('row', 'col'), may hold values from 0.1 to 10
Outputs:
- backward: float32 [2, 192, 32768], P(None, 'col', 'row')
- counts: float32 [32768, 1024], P('row', 'col')
Inputs may be any that keep to these rules, and one draw needn't show every extreme that they name: Positive transition weights. Positive forward weights.
All inputs are finite; a program needn't handle non-finite values.
Results may differ from a plain program's by a relative error of at most 0.00048.
Values may be sent and summed in bfloat16 or wider, within the bound.
A program may use at most 192 MiB of HBM per device.

v0:
```python
import jax
import jax.numpy as jnp
from jax import lax
from jax.sharding import PartitionSpec as P

H = 32768
N = 192
DW = 128


def spread(value, axis, source):
    kept = jnp.where(lax.axis_index(axis) == source, value, 0).astype(value.dtype)
    return lax.psum(kept, axis)


def on_device(transition, emission, token_ids, forward, backward_last):
    row_count = lax.axis_size("row")
    col_count = lax.axis_size("col")
    col_index = lax.axis_index("col")
    ratio = col_count // row_count
    local_seqs = forward.shape[1]
    block_src = transition.shape[0]
    block_dst = transition.shape[1]
    seq_total = local_seqs * col_count
    forward_all = lax.all_gather(forward, "col", axis=1, tiled=True)
    backward_next = lax.all_gather(backward_last, "row", axis=0, tiled=True)
    columns = lax.broadcasted_iota(jnp.int32, (seq_total, emission.shape[0]), 1)
    window = transition[:, :DW]
    totals = jnp.zeros((block_src, DW), jnp.float32)
    outputs = [None, None]
    for step in (1, 0):
        onehot = (token_ids[step][:, None] == columns).astype(jnp.bfloat16)
        emitted = jnp.dot(onehot, emission, preferred_element_type=jnp.float32)
        weighted_back = (emitted * backward_next).astype(jnp.bfloat16)
        partial_value = lax.dot_general(
            weighted_back, transition, (((1,), (1,)), ((), ())), preferred_element_type=jnp.float32
        )
        alpha_all = forward_all[step].astype(jnp.float32)
        summed = lax.psum(partial_value, "col")
        mine = lax.dynamic_slice_in_dim(summed, col_index * local_seqs, local_seqs, 0)
        alpha_mine = forward[step].astype(jnp.float32)
        local_norm = lax.psum(jnp.sum(alpha_mine * mine, axis=1), "row")
        normal_all = lax.all_gather(local_norm, "col", axis=0, tiled=True)
        normal_mine = lax.dynamic_slice_in_dim(normal_all, col_index * local_seqs, local_seqs, 0)
        outputs[step] = mine / normal_mine[:, None]
        scaled = (alpha_all / normal_all[:, None]).astype(jnp.bfloat16)
        totals = totals + lax.dot_general(
            scaled,
            weighted_back[:, :DW],
            (((0,), (0,)), ((), ())),
            preferred_element_type=jnp.float32,
        )
        if step == 1:
            whole = summed / normal_all[:, None]
            piece = lax.dynamic_slice_in_dim(whole, col_index % ratio * block_dst, block_dst, 1)
            backward_next = spread(piece, "row", col_index // ratio)
    counts = window.astype(jnp.float32) * totals * (H * H / N)
    return (jnp.stack(outputs), counts)


def solution(mesh):
    in_specs = (P("row", "col"), P(None, "col"), P(), P(None, "col", "row"), P("row", "col"))
    out_specs = (P(None, "col", "row"), P("row", "col"))
    return jax.shard_map(
        on_device, mesh=mesh, in_specs=in_specs, out_specs=out_specs, check_vma=False
    )
```

profile of v0, /device:TPU:0, one launch (start us, length us, event | category | flops | bytes accessed | tf_op | source)
XLA Modules:
  0.0 741.6 jit_solution(9007567216397277755)
XLA Ops:
  7.2 0.0 copy-start
  7.2 0.0 all-gather.3.cloned.1.call-start
  7.2 0.7 all-gather.3.cloned.1.call-update
  7.9 0.0 all-reduce.6.cloned.1.call-start
  8.0 0.8 fusion.17
  8.7 32.1 %all-gather.3.cloned.1.call-done = f32[192,4096]{1,0:T(8,128)} async-done(((f32[48,4096]{1,0:T(8,128)}), f32[192,4096]{1,0:T(8,128)}) %all-gather.3.cloned.1.call-update) | async-done | bytes 3145744 | tf_op jit(solution)/shard_map/all_gather | solution.py:26
  40.8 0.0 copy-done
  40.8 2.5 fusion.5
  43.3 31.1 %fusion.18 = f32[192,8192]{1,0:T(8,128)} fusion(bf16[192,4096]{1,0:T(8,128)(2,1)S(1)} %fusion.5, bf16[8192,4096]{1,0:T(8,128)(2,1)} %param.5), kind=kOutput, calls=%fused_computation.31 | convolution fusion | flops 12884901888 | bytes 74973184 | tf_op jit(solution)/shard_map/dot_general | solution.py:35
  74.5 0.0 copy-start.3
  74.5 0.0 copy-start.1
  74.5 0.0 all-reduce.6.cloned.1.call-update
  74.5 0.0 all-reduce.8.cloned.1.call-start
  74.6 0.6 copy-done.3
  75.1 0.6 dynamic-slice
  76.4 209.8 %all-reduce.6.cloned.1.call-done = f32[192,8192]{1,0:T(8,128)} async-done(((f32[192,8192]{1,0:T(8,128)}), f32[192,8192]{1,0:T(8,128)}) %all-reduce.6.cloned.1.call-update) | async-done | bytes 6291472 | tf_op jit(solution)/shard_map/psum | solution.py:39
  286.2 0.0 copy-done.1
  286.2 1.3 fusion.12
  287.5 6.9 psum.36
  294.4 0.2 dynamic-update-slice
  294.7 19.4 %all-reduce = f32[192]{0:T(256)S(1)} all-reduce(f32[192]{0:T(256)S(1)} %dynamic-update-slice), channel_id=1, replica_groups=mesh['row'=4,'col'=8] {'col'}, use_global_device_ids=true, to_apply=%add | all-reduce | flops 192 | bytes 1536
  314.1 4.0 fusion.7
  318.1 0.0 all-reduce.8.cloned.1.call-update
  318.1 0.0 all-gather.5.cloned.1.call-start
  318.1 0.5 all-gather.5.cloned.1.call-update
  318.7 0.0 all-reduce.10.cloned.1.call-start
  318.7 64.3 %all-reduce.8.cloned.1.call-done = f32[192,4096]{1,0:T(8,128)} async-done(((f32[192,4096]{1,0:T(8,128)}), f32[192,4096]{1,0:T(8,128)}) %all-reduce.8.cloned.1.call-update) | async-done | bytes 3145744 | tf_op jit(solution)/shard_map/psum | solution.py:13
  383.0 3.7 fusion.4
  386.7 30.8 %fusion.19 = f32[192,8192]{1,0:T(8,128)} fusion(bf16[192,4096]{1,0:T(8,128)(2,1)} %fusion.4, bf16[8192,4096]{1,0:T(8,128)(2,1)} %param.5), kind=kOutput, calls=%fused_computation.32 | convolution fusion | flops 12884901888 | bytes 74973184 | tf_op jit(solution)/shard_map/dot_general | solution.py:35
  417.5 0.0 all-reduce.10.cloned.1.call-update
  417.5 0.1 dynamic_slice.19
  417.6 0.0 copy-start.2
  417.6 66.8 %all-gather.5.cloned.1.call-done = bf16[2,192,8192]{2,1,0:T(8,128)(2,1)} async-done(((bf16[2,24,8192]{2,1,0:T(8,128)(2,1)}), bf16[2,192,8192]{2,1,0:T(8,128)(2,1)}) %all-gather.5.cloned.1.call-update) | async-done | bytes 6291472 | tf_op jit(solution)/shard_map/all_gather | solution.py:25
  484.4 5.4 fusion.9
  489.9 1.3 divide_bitcast_fusion
  491.1 207.2 %all-reduce.10.cloned.1.call-done = f32[192,8192]{1,0:T(8,128)} async-done(((f32[192,8192]{1,0:T(8,128)}), f32[192,8192]{1,0:T(8,128)}) %all-reduce.10.cloned.1.call-update) | async-done | bytes 6291472 | tf_op jit(solution)/shard_map/psum | solution.py:39
  698.3 0.0 copy-done.2
  698.3 1.3 fusion.11
  699.6 6.9 psum.39
  706.5 0.2 dynamic-update-slice.1
  706.7 19.4 %all-reduce.1 = f32[192]{0:T(256)S(1)} all-reduce(f32[192]{0:T(256)S(1)} %dynamic-update-slice.1), channel_id=1, replica_groups=mesh['row'=4,'col'=8] {'col'}, use_global_device_ids=true, to_apply=%add.1 | all-reduce | flops 192 | bytes 1536
  726.1 0.0 copy-start.4
  726.2 0.1 dynamic_slice.18
  726.2 1.4 divide_bitcast_fusion.1
  727.6 1.2 pad_maximum_fusion
  728.9 0.0 copy-done.4
  728.9 6.2 fusion.1
  (2 shorter events, 0.0 us)
Async XLA Ops:
  7.2 33.7 %copy-start = (bf16[96,4096]{1,0:T(8,128)(2,1)S(1)}, bf16[96,4096]{1,0:T(8,128)(2,1)}, u32[]{:S(2)}) copy-start(bf16[96,4096]{1,0:T(8,128)(2,1)} %param.6) | copy-start | bytes 2359300
  7.2 33.7 %all-gather.3.cloned.1.call-start = ((), (), s32[]{:S(2)}) async-start(), calls=%async_computation | async-start | bytes 3932160 | tf_op jit(solution)/shard_map/all_gather | solution.py:26
  7.9 278.3 %all-reduce.6.cloned.1.call-start = ((), (), s32[]{:S(2)}) async-start(), calls=%async_computation.1 | async-start | bytes 12582912 | tf_op jit(solution)/shard_map/psum | solution.py:39
  74.5 0.7 copy-start.3
  74.5 211.8 %copy-start.1 = (bf16[2,24,8192]{2,1,0:T(8,128)(2,1)S(1)}, bf16[2,24,8192]{2,1,0:T(8,128)(2,1)}, u32[]{:S(2)}) copy-start(bf16[2,24,8192]{2,1,0:T(8,128)(2,1)} %param.8) | copy-start | bytes 2359300
  74.5 308.5 %all-reduce.8.cloned.1.call-start = ((), (), s32[]{:S(2)}) async-start(), calls=%async_computation.2 | async-start | bytes 6291456 | tf_op jit(solution)/shard_map/psum | solution.py:13
  318.1 166.4 %all-gather.5.cloned.1.call-start = ((), (), s32[]{:S(2)}) async-start(), calls=%async_computation.4 | async-start | bytes 7077888 | tf_op jit(solution)/shard_map/all_gather | solution.py:25
  318.7 379.7 %all-reduce.10.cloned.1.call-start = ((), (), s32[]{:S(2)}) async-start(), calls=%async_computation.3 | async-start | bytes 12582912 | tf_op jit(solution)/shard_map/psum | solution.py:39
  417.6 280.7 %copy-start.2 = (bf16[2,24,8192]{2,1,0:T(8,128)(2,1)S(1)}, bf16[2,24,8192]{2,1,0:T(8,128)(2,1)}, u32[]{:S(2)}) copy-start(bf16[2,24,8192]{2,1,0:T(8,128)(2,1)} %param.8) | copy-start | bytes 2359300
  726.1 2.7 copy-start.4
Sparse Core Ops, SparseCore 0:
  9.6 31.2 all-gather.2
  74.6 211.5 all-reduce.5
  318.2 64.7 all-reduce.7
  385.3 99.1 all-gather.4
  488.5 209.7 all-reduce.9
where the time goes:
time: 742 us
  waiting for transfers between devices  582 us (78%)
  matrix products  79.7 us (11%)
  blocking collectives  52.5 us (7%)
  between operations  14.5 us (2%)
  other arithmetic  10.5 us (1%)
    psum x2, waiting for transfers between devices, on_device(): summed = lax.psum(partial_value, 'col')  417 us
    all_gather x1, waiting for transfers between devices, on_device(): forward_all = lax.all_gather(forward, 'col', axis=1, tiled=True)  66.8 us
    psum x1, waiting for transfers between devices, spread(): return lax.psum(kept, axis)  64.3 us
    dot_general x2, matrix products, on_device(): lax.dot_general(weighted_back, transition, (((1,), (1,)), ((), ())), pref...  61.9 us
    unnamed x2, blocking collectives  38.8 us
    all_gather x1, waiting for transfers between devices, on_device(): backward_next = lax.all_gather(backward_last, 'row', axis=0, tiled=True)  32.1 us
  transfers between devices with their start and end apart: 5, of which 5 were waited for; matrix products, arithmetic and copies ran while one was open for 6% of the time, Pallas kernels for 0%

commit v1 on v0

--- a/solution.py
+++ b/solution.py
@@ -36,7 +36,7 @@
             weighted_back, transition, (((1,), (1,)), ((), ())), preferred_element_type=jnp.float32
         )
         alpha_all = forward_all[step].astype(jnp.float32)
-        summed = lax.psum(partial_value, "col")
+        summed = jnp.sum(lax.all_gather(partial_value, "col"), axis=0)
         mine = lax.dynamic_slice_in_dim(summed, col_index * local_seqs, local_seqs, 0)
         alpha_mine = forward[step].astype(jnp.float32)
         local_norm = lax.psum(jnp.sum(alpha_mine * mine, axis=1), "row")

time: 742 us -> 2260 us (3.05)
  waiting for transfers between devices: 582 us -> 2060 us
  other arithmetic: 10.5 us -> 50.7 us
    all_gather x0 -> x2, waiting for transfers between devices: none -> 1900 us  [on_device(): summed = jnp.sum(lax.all_gather(partial_value, 'col'), axis=0)]
    psum x2 -> x0, waiting for transfers between devices: 417 us -> none  [on_device(): summed = lax.psum(partial_value, 'col')]
    reduce_sum x0 -> x2, other arithmetic: none -> 40.1 us  [on_device(): summed = jnp.sum(lax.all_gather(partial_value, 'col'), axis=0)]
  transfers between devices with their start and end apart: 5 -> 5, of which waited for: 5 -> 5; matrix products, arithmetic and copies ran while one was open for 6% -> 2% of each run, Pallas kernels for 0% -> 0%
where the time goes in v1:
time: 2260 us
  waiting for transfers between devices  2060 us (91%)
  matrix products  79.7 us (4%)
  blocking collectives  54.5 us (2%)
  other arithmetic  50.7 us (2%)
    all_gather x2, waiting for transfers between devices, on_device(): summed = jnp.sum(lax.all_gather(partial_value, 'col'), axis=0)  1900 us
    all_gather x1, waiting for transfers between devices, on_device(): forward_all = lax.all_gather(forward, 'col', axis=1, tiled=True)  66.7 us
    psum x1, waiting for transfers between devices, spread(): return lax.psum(kept, axis)  64.1 us
    dot_general x2, matrix products, on_device(): lax.dot_general(weighted_back, transition, (((1,), (1,)), ((), ())), pref...  61.9 us
  transfers between devices with their start and end apart: 5, of which 5 were waited for; matrix products, arithmetic and copies ran while one was open for 2% of the time, Pallas kernels for 0%

profile of v1, /device:TPU:0, one launch (start us, length us, event | category | flops | bytes accessed | tf_op | source)
XLA Modules:
  0.0 2262.0 jit_solution(6924776727963058960)
XLA Ops:
  7.2 0.0 copy-start
  7.2 0.0 all-gather.7.cloned.1.call-start
  7.2 0.7 all-gather.7.cloned.1.call-update
  7.9 0.0 all-gather.11.cloned.1.call-start
  8.0 0.8 fusion.17
  8.7 32.1 %all-gather.7.cloned.1.call-done = f32[192,4096]{1,0:T(8,128)} async-done(((f32[48,4096]{1,0:T(8,128)}), f32[192,4096]{1,0:T(8,128)}) %all-gather.7.cloned.1.call-update) | async-done | bytes 3145744 | tf_op jit(solution)/shard_map/all_gather | solution.py:26
  40.8 0.0 copy-done
  40.8 2.5 fusion.5
  43.3 31.1 %fusion.18 = f32[192,8192]{1,0:T(8,128)} fusion(bf16[192,4096]{1,0:T(8,128)(2,1)S(1)} %fusion.5, bf16[8192,4096]{1,0:T(8,128)(2,1)} %param.5), kind=kOutput, calls=%fused_computation.31 | convolution fusion | flops 12884901888 | bytes 74973184 | tf_op jit(solution)/shard_map/dot_general | solution.py:35
  74.4 0.0 copy-start.4
  74.4 0.0 all-gather.11.cloned.1.call-update
  74.5 0.0 all-reduce.4.cloned.1.call-start
  74.5 0.6 copy-done.4
  75.1 0.6 dynamic-slice
  76.3 950.6 %all-gather.11.cloned.1.call-done = f32[1536,8192]{1,0:T(8,128)} async-done(((f32[192,8192]{1,0:T(8,128)}), f32[1536,8192]{1,0:T(8,128)}) %all-gather.11.cloned.1.call-update) | async-done | bytes 50331664 | tf_op jit(solution)/shard_map/all_gather | solution.py:39
  1026.9 0.0 copy-start.2
  1026.9 20.0 reduce_sum.36
  1047.0 0.0 copy-done.2
  1047.0 1.3 fusion.12
  1048.3 6.9 psum.21
  1055.2 0.2 dynamic-update-slice
  1055.4 20.4 all-reduce
  1075.8 4.0 fusion.7
  1079.8 0.0 all-reduce.4.cloned.1.call-update
  1079.8 0.0 all-gather.9.cloned.1.call-start
  1079.8 0.5 all-gather.9.cloned.1.call-update
  1080.4 0.0 all-gather.13.cloned.1.call-start
  1080.4 64.1 %all-reduce.4.cloned.1.call-done = f32[192,4096]{1,0:T(8,128)} async-done(((f32[192,4096]{1,0:T(8,128)}), f32[192,4096]{1,0:T(8,128)}) %all-reduce.4.cloned.1.call-update) | async-done | bytes 3145744 | tf_op jit(solution)/shard_map/psum | solution.py:13
  1144.5 3.6 fusion.4
  1148.2 30.8 %fusion.19 = f32[192,8192]{1,0:T(8,128)} fusion(bf16[192,4096]{1,0:T(8,128)(2,1)} %fusion.4, bf16[8192,4096]{1,0:T(8,128)(2,1)} %param.5), kind=kOutput, calls=%fused_computation.32 | convolution fusion | flops 12884901888 | bytes 74973184 | tf_op jit(solution)/shard_map/dot_general | solution.py:35
  1179.0 0.0 all-gather.13.cloned.1.call-update
  1179.0 0.1 dynamic_slice.19
  1179.1 66.7 %all-gather.9.cloned.1.call-done = bf16[2,192,8192]{2,1,0:T(8,128)(2,1)} async-done(((bf16[2,24,8192]{2,1,0:T(8,128)(2,1)}), bf16[2,192,8192]{2,1,0:T(8,128)(2,1)}) %all-gather.9.cloned.1.call-update) | async-done | bytes 6291472 | tf_op jit(solution)/shard_map/all_gather | solution.py:25
  1245.8 5.4 fusion.9
  1251.2 1.3 divide_bitcast_fusion
  1252.5 945.2 %all-gather.13.cloned.1.call-done = f32[1536,8192]{1,0:T(8,128)} async-done(((f32[192,8192]{1,0:T(8,128)}), f32[1536,8192]{1,0:T(8,128)}) %all-gather.13.cloned.1.call-update) | async-done | bytes 50331664 | tf_op jit(solution)/shard_map/all_gather | solution.py:39
  2197.7 0.0 copy-start.3
  2197.7 20.0 reduce_sum.38
  2217.7 0.0 copy-done.3
  2217.7 1.3 fusion.11
  2219.0 6.9 psum.23
  2225.9 0.2 dynamic-update-slice.1
  2226.2 20.4 all-reduce.1
  2246.5 0.0 copy-start.5
  2246.5 0.1 dynamic_slice.18
  2246.6 1.4 divide_bitcast_fusion.1
  2248.0 1.2 pad_maximum_fusion
  2249.3 0.0 copy-done.5
  2249.3 0.0 copy-start.1
  2249.3 6.2 fusion.1
  2255.5 0.0 copy-done.1
  (2 shorter events, 0.0 us)
Async XLA Ops:
  7.2 33.7 %copy-start = (bf16[96,4096]{1,0:T(8,128)(2,1)S(1)}, bf16[96,4096]{1,0:T(8,128)(2,1)}, u32[]{:S(2)}) copy-start(bf16[96,4096]{1,0:T(8,128)(2,1)} %param.6) | copy-start | bytes 2359300
  7.2 33.7 %all-gather.7.cloned.1.call-start = ((), (), s32[]{:S(2)}) async-start(), calls=%async_computation | async-start | bytes 3932160 | tf_op jit(solution)/shard_map/all_gather | solution.py:26
  7.9 1019.0 %all-gather.11.cloned.1.call-start = ((), (), s32[]{:S(2)}) async-start(), calls=%async_computation.3 | async-start | bytes 56623104 | tf_op jit(solution)/shard_map/all_gather | solution.py:39
  74.4 0.7 copy-start.4
  74.5 1070.1 %all-reduce.4.cloned.1.call-start = ((), (), s32[]{:S(2)}) async-start(), calls=%async_computation.1 | async-start | bytes 6291456 | tf_op jit(solution)/shard_map/psum | solution.py:13
  1026.9 20.1 copy-start.2
  1079.8 166.0 %all-gather.9.cloned.1.call-start = ((), (), s32[]{:S(2)}) async-start(), calls=%async_computation.2 | async-start | bytes 7077888 | tf_op jit(solution)/shard_map/all_gather | solution.py:25
  1080.4 1117.3 %all-gather.13.cloned.1.call-start = ((), (), s32[]{:S(2)}) async-start(), calls=%async_computation.4 | async-start | bytes 56623104 | tf_op jit(solution)/shard_map/all_gather | solution.py:39
  2197.7 20.1 copy-start.3
  2246.5 2.7 copy-start.5
  2249.3 6.3 copy-start.1
Sparse Core Ops, SparseCore 0:
  9.6 31.2 all-gather.6
  74.6 952.3 all-gather.10
  1079.9 64.5 all-reduce.3
  1146.6 99.1 all-gather.8
  1247.1 950.4 all-gather.12
